TPU v7x, 32 devices: a whole 2x2x4 slice. The times are simulated.
32 devices in a mesh: batch: 4 (over y, core), lat: 8 (over z, x).
Axes of the slice: x: 2, y: 2, z: 4, core: 2. Of those that a mesh axis runs over, the one named last changes fastest.
Arguments:
- adjoint_in: float32 [80, 60, 16, 128], P('batch', None, 'lat'), may hold values from -6 to 6
- east_courant: bfloat16 [4, 60, 16, 128], P('batch', None, 'lat'), may hold values from -0.8984375 to 0.8984375
- north_courant: bfloat16 [4, 60, 16, 128], P('batch', None, 'lat'), may hold values from -0.8984375 to 0.8984375
- convection: bfloat16 [4, 60, 60, 16, 128], P('batch', None, None, 'lat'), may hold values from 0 to 1, as said below
- hour_owner: int32 [4, 16], P(None, 'lat'), may hold values from 0 to 3, as said below
- obs_lat: int32 [80], P('batch'), may hold values from 0 to 15
- obs_lon: int32 [80], P('batch'), may hold values from 0 to 127
- obs_level: int32 [80], P('batch'), may hold values from 0 to 59
- obs_hour: int32 [80], P('batch'), may hold values from 0 to 1
- misfit: float32 [80], P('batch'), may hold values from -8 to 8
Outputs:
- adjoint_out: float32 [80, 60, 16, 128], P('batch', None, 'lat')
- emission_grad: float32 [16, 128], P('lat')
Inputs may be any that keep to these rules, and one draw needn't show every extreme that they name: Each column hour_owner[:, y] names every slot once; the 2 rows of one latitude device share their column. `convection`: nonnegative entries.
All inputs are finite; a program needn't handle non-finite values.
Results may differ from a plain program's by a relative error of at most 0.0039.
Values may be sent and summed in bfloat16 or wider, within the bound.
A program may use at most 128 MiB of HBM per device.

v0:
```python
import math

import jax
import jax.numpy as jnp
from jax import lax
from jax.sharding import PartitionSpec as P

HOURS = 2


def with_halo(shard, sides, width):
    for axis, dim in sides:
        size, length = (lax.axis_size(axis), shard.shape[dim])
        up = [(i, (i + 1) % size) for i in range(size - 1)]
        down = [(j, i) for i, j in up]
        last = lax.slice_in_dim(shard, length - width, length, axis=dim)
        initial = lax.slice_in_dim(shard, 0, width, axis=dim)
        before = lax.ppermute(last, axis, up)
        after = lax.ppermute(initial, axis, down)
        shard = jnp.concatenate([before, shard, after], axis=dim)
    return shard


def broadcast(value, axis, source):
    kept = jnp.where(lax.axis_index(axis) == source, value, 0).astype(value.dtype)
    return lax.psum(kept, axis)


def coefficients(courant):
    pos_part = jnp.maximum(courant, 0.0)
    neg_part = jnp.minimum(courant, 0.0)
    return (
        pos_part,
        neg_part,
        pos_part * (1.0 - pos_part) * 0.5,
        neg_part * (1.0 + neg_part) * 0.5,
    )


def cut_range(array, begin, end, axis):
    return lax.slice_in_dim(array, begin, end, axis=axis)


def adjoint_core(padded, courant, axis, count):
    jump = cut_range(padded, 1, count + 4, axis) - cut_range(padded, 0, count + 3, axis)
    pos_part, neg_part, pos_term, neg_term = coefficients(cut_range(courant, 0, count + 3, axis))
    slope_terms = cut_range(pos_term, 1, count + 3, axis) * cut_range(
        jump, 1, count + 3, axis
    ) - cut_range(neg_term, 0, count + 2, axis) * cut_range(jump, 0, count + 2, axis)
    result = cut_range(padded, 2, count + 2, axis)
    result = result + cut_range(pos_part, 2, count + 2, axis) * cut_range(jump, 2, count + 2, axis)
    result = result + cut_range(neg_part, 1, count + 1, axis) * cut_range(jump, 1, count + 1, axis)
    return result + 0.5 * (
        cut_range(slope_terms, 0, count, axis) - cut_range(slope_terms, 2, count + 2, axis)
    )


def zero_pad(array, axis):
    widths = [(0, 0)] * array.ndim
    widths[axis] = (2, 2)
    return jnp.pad(array, widths)


def latitude_sweep(adjoint, north):
    tracers = adjoint.shape[0]
    count = adjoint.shape[2]
    stacked = jnp.concatenate([adjoint, north[None]], axis=0)
    padded = with_halo(stacked, (("lat", 2),), 1)
    field = padded[:tracers]
    courant = padded[tracers:]
    jump = cut_range(field, 1, count + 2, 2) - cut_range(field, 0, count + 1, 2)
    pos_part, neg_part, pos_term, neg_term = coefficients(courant)
    slope_terms = cut_range(pos_term, 1, count + 1, 2) * cut_range(
        jump, 1, count + 1, 2
    ) - cut_range(neg_term, 0, count, 2) * cut_range(jump, 0, count, 2)
    slope_pad = with_halo(slope_terms, (("lat", 2),), 1)
    result = cut_range(field, 1, count + 1, 2)
    result = result + cut_range(pos_part, 1, count + 1, 2) * cut_range(jump, 1, count + 1, 2)
    result = result + cut_range(neg_part, 0, count, 2) * cut_range(jump, 0, count, 2)
    return result + 0.5 * (
        cut_range(slope_pad, 0, count, 2) - cut_range(slope_pad, 2, count + 2, 2)
    )


def fetch(convection, east_courant, north_courant, hour_owner, hour):
    return (
        broadcast(convection[0], "batch", hour_owner[hour, 0]),
        broadcast(east_courant[0], "batch", hour_owner[hour, 0]),
        broadcast(north_courant[0], "batch", hour_owner[hour, 0]),
    )


def on_device(
    adjoint_in,
    east_courant,
    north_courant,
    convection,
    hour_owner,
    obs_lat,
    obs_lon,
    obs_level,
    obs_hour,
    misfit,
):
    tracers, levels, rows, width = adjoint_in.shape
    first = lax.axis_index("lat") * rows
    last_row = lax.axis_size("lat") * rows - 1
    lev_ids = lax.broadcasted_iota(jnp.int32, (1, levels, 1, 1), 1)
    row_ids = first + lax.broadcasted_iota(jnp.int32, (1, 1, rows, 1), 2)
    lon_ids = lax.broadcasted_iota(jnp.int32, (1, 1, 1, width), 3)
    north_rows = first + lax.broadcasted_iota(jnp.int32, (1, rows, 1), 1)
    scale = 1.0 / math.sqrt(tracers * lax.axis_size("batch"))
    adjoint = adjoint_in
    grad = jnp.zeros((rows, width), jnp.float32)
    for hour in reversed(range(HOURS)):
        met = fetch(convection, east_courant, north_courant, hour_owner, hour)
        hour_adjoint = adjoint
        mixing, east, north = met
        hit = (lev_ids == obs_level[:, None, None, None]) & (
            row_ids == obs_lat[:, None, None, None]
        )
        hit = (
            hit
            & (lon_ids == obs_lon[:, None, None, None])
            & (obs_hour[:, None, None, None] == hour)
        )
        hour_adjoint = hour_adjoint + jnp.where(hit, misfit[:, None, None, None], 0.0)
        east = east.astype(jnp.float32)
        north = jnp.where(north_rows == last_row, 0.0, north.astype(jnp.float32))
        hour_adjoint = adjoint_core(zero_pad(hour_adjoint, 3), zero_pad(east[None], 3), 3, width)
        hour_adjoint = latitude_sweep(hour_adjoint, north)
        rounded = hour_adjoint.astype(jnp.bfloat16)
        hour_adjoint = jnp.einsum(
            "mkyx,tmyx->tkyx", mixing, rounded, preferred_element_type=jnp.float32
        )
        adjoint, grad = (hour_adjoint, grad + jnp.sum(hour_adjoint[:, 0], axis=0))
    total = lax.psum(grad, "batch")
    return (adjoint, total * scale)


def solution(mesh):
    return jax.shard_map(
        on_device,
        mesh=mesh,
        in_specs=(
            P("batch", None, "lat", None),
            P("batch", None, "lat", None),
            P("batch", None, "lat", None),
            P("batch", None, None, "lat", None),
            P(None, "lat"),
            P("batch"),
            P("batch"),
            P("batch"),
            P("batch"),
            P("batch"),
        ),
        out_specs=(P("batch", None, "lat", None), P("lat", None)),
        check_vma=False,
    )
```

profile of v0, /device:TPU:9, one launch (start us, length us, event | category | flops | bytes accessed | tf_op | source)
XLA Modules:
  0.0 372.0 jit_solution(11669923439552679015)
XLA Ops:
  13.0 7.1 %copy.87 = bf16[1,60,60,2,128]{2,1,4,3,0:T(8,128)(2,1)} copy(bf16[1,60,60,2,128]{4,3,2,1,0:T(2,128)(2,1)} %param.13) | data formatting | bytes 3686400 | tf_op args[3]
  20.8 2.8 copy.71
  27.0 18.6 %all-reduce.9.cloned.1.call-done = (bf16[1,60,2,128]{1,3,2,0:T(8,128)(2,1)}, bf16[60,2,128]{0,2,1:T(8,128)(2,1)}, bf16[1,60,2,128]{1,3,2,0:T(8,128)(2,1)}, bf16[60,2,128]{0,2,1:T(8,128)(2,1)}) async-done(((bf16[1,60,2,128]{1,3,2,0:T(8,128)(2,1)}, bf16[60,2,128]{0,2,1:T(8,128)(2,1)}, bf16[1,60,2,128]{1,3,2,0:T(8,128)(2,1)}, bf16[60,2,128]{0,2,1:T(8,128)(2,1)}), (bf16[1,60,2,128]{1,3,2,0:T(8,128)(2,1)}, ...) | async-done | bytes 122896 | tf_op jit(solution)/shard_map/psum | solution.py:26
  49.3 5.0 %fusion.17 = f32[20,60,2,128]{1,0,3,2:T(8,128)S(1)} fusion(f32[20,60,2,130]{1,0,3,2:T(8,128)S(1)} %fusion.3, f32[20,60,2,131]{1,0,3,2:T(8,128)} %copy-done, f32[60,2,128]{0,2,1:T(8,128)S(1)} %slice_bitcast_fusion.2, f32[60,2,128]{0,2,1:T(8,128)S(1)} %slice_bitcast_fusion.3, f32[20,60,2,128]{1,0,3,2:T(8,128)S(1)} %copy-done.6, f32[20]{0:T(128)S(1)} %copy-done.19, ...), kind=kLoop, calls=%fused_computation.51 | loop fusion | flops 3379200 | bytes 7500740 | tf_op jit(solution)/shard_map/add | solution.py:53
  56.4 3.3 copy.74
  59.8 3.1 collective-permute-start
  62.8 3.3 copy.75
  66.2 3.1 collective-permute-start.1
  69.2 6.0 %select_bitcast_fusion.1 = (bf16[60,60,2,128]{1,0,3,2:T(8,128)(2,1)}, bf16[60,60,2,128]{1,0,3,2:T(8,128)(2,1)}) fusion(bf16[1,60,60,2,128]{2,1,4,3,0:T(8,128)(2,1)} %copy.87, pred[]{:T(512)S(6)} %eq.112, pred[]{:T(512)S(6)} %eq.115), kind=kLoop, calls=%fused_computation.17 | loop fusion | flops 1843200 | bytes 5529602 | tf_op jit(solution)/shard_map/jit(_where)/select_n | solution.py:25
  77.2 4.2 %copy.76 = f32[21,60,2,128]{3,2,1,0:T(2,128)} copy(f32[21,60,2,128]{1,0,3,2:T(8,128)} %pad_maximum_fusion) | data formatting | bytes 2580480 | tf_op jit(solution)/shard_map/concatenate | solution.py:67
  83.1 6.0 %collective-permute-done = f32[21,60,1,128]{3,2,1,0:T(1,128)} collective-permute-done((f32[21,60,1,128]{3,2,1,0:T(1,128)}, f32[21,60,1,128]{3,2,1,0:T(1,128)}, u32[]{:S(2)}, u32[]{:S(2)}) %collective-permute-start) | collective-permute-done | bytes 645152 | tf_op jit(solution)/shard_map/ppermute | solution.py:18
  89.1 4.0 %collective-permute-done.1 = f32[21,60,1,128]{3,2,1,0:T(1,128)} collective-permute-done((f32[21,60,1,128]{3,2,1,0:T(1,128)}, f32[21,60,1,128]{3,2,1,0:T(1,128)}, u32[]{:S(2)}, u32[]{:S(2)}) %collective-permute-start.1) | collective-permute-done | bytes 645152 | tf_op jit(solution)/shard_map/ppermute | solution.py:19
  98.7 3.3 copy.79
  101.9 3.3 copy.78
  105.2 2.6 fusion.1
  110.0 2.1 fusion.51
  112.7 3.3 copy.85
  117.9 3.4 copy.83
  121.3 3.5 collective-permute-start.2
  129.6 16.6 %collective-permute-done.3 = f32[20,60,1,128]{3,2,1,0:T(1,128)} collective-permute-done((f32[20,60,1,128]{3,2,1,0:T(1,128)}, f32[20,60,1,128]{3,2,1,0:T(1,128)}, u32[]{:S(2)}, u32[]{:S(2)}) %collective-permute-start.3) | collective-permute-done | bytes 614432 | tf_op jit(solution)/shard_map/ppermute | solution.py:19
  146.2 3.3 copy.86
  149.5 3.3 copy.84
  152.8 77.2 %all-reduce.11.cloned.1.call-done = (bf16[60,60,2,128]{1,0,3,2:T(8,128)(2,1)}, bf16[60,60,2,128]{1,0,3,2:T(8,128)(2,1)}) async-done(((bf16[60,60,2,128]{1,0,3,2:T(8,128)(2,1)}, bf16[60,60,2,128]{1,0,3,2:T(8,128)(2,1)}), (bf16[60,60,2,128]{1,0,3,2:T(8,128)(2,1)}, bf16[60,60,2,128]{1,0,3,2:T(8,128)(2,1)})) %all-reduce.11.cloned.1.call-update) | async-done | bytes 3686416 | tf_op jit(solution)/shard_map/psum | solution.py:26
  230.0 10.5 %select_add_fusion = (f32[20,60,2,128]{1,0,3,2:T(8,128)}, f32[20,60,2,128]{1,0,3,2:T(8,128)}) fusion(f32[20]{0:T(128)} %param.19, pred[20]{0:T(512)(128)(4,1)} %get-tuple-element.48, pred[20,128]{0,1:T(8,128)(4,1)} %copy-done.14, pred[20,60,2]{1,0,2:T(8,128)(4,1)S(1)} %broadcast_and_fusion, bf16[60,60,2,128]{1,0,3,2:T(8,128)(2,1)} %get-tuple-element.13, ...), kind=kOutput, calls=%fused_computation.57 | convolution fusion | flops 41164800 | bytes 20675936 | tf_op jit(solution)/shard_map/mkyx,tmyx->tkyx/dot_general | solution.py:133
  240.5 3.3 slice_subtract_fusion
  246.7 2.0 fusion.21
  248.7 3.3 copy.91
  252.0 3.1 collective-permute-start.4
  255.1 3.3 copy.92
  258.4 3.1 collective-permute-start.5
  261.5 2.0 pad_maximum_fusion.1
  263.5 4.2 %copy.93 = f32[21,60,2,128]{3,2,1,0:T(2,128)} copy(f32[21,60,2,128]{1,0,3,2:T(8,128)} %pad_maximum_fusion.1) | data formatting | bytes 2580480 | tf_op jit(solution)/shard_map/concatenate | solution.py:67
  267.8 14.5 %collective-permute-done.4 = f32[21,60,1,128]{3,2,1,0:T(1,128)} collective-permute-done((f32[21,60,1,128]{3,2,1,0:T(1,128)}, f32[21,60,1,128]{3,2,1,0:T(1,128)}, u32[]{:S(2)}, u32[]{:S(2)}) %collective-permute-start.4) | collective-permute-done | bytes 645152 | tf_op jit(solution)/shard_map/ppermute | solution.py:18
  282.2 3.1 collective-permute-done.5
  289.6 3.4 copy.96
  293.0 3.3 copy.95
  296.2 2.5 fusion
  303.5 3.3 copy.102
  306.8 2.0 collective-permute-start.7
  308.8 3.3 copy.100
  312.1 3.6 collective-permute-start.6
  315.7 2.9 slice_reduce_fusion.1
  318.9 18.3 %collective-permute-done.7 = f32[20,60,1,128]{3,2,1,0:T(1,128)} collective-permute-done((f32[20,60,1,128]{3,2,1,0:T(1,128)}, f32[20,60,1,128]{3,2,1,0:T(1,128)}, u32[]{:S(2)}, u32[]{:S(2)}) %collective-permute-start.7) | collective-permute-done | bytes 614432 | tf_op jit(solution)/shard_map/ppermute | solution.py:19
  337.2 3.2 copy.103
  340.4 3.3 copy.101
  343.7 9.1 %convolution_bitcast_fusion = f32[20,60,2,128]{1,0,3,2:T(8,128)} fusion(bf16[60,60,2,128]{1,0,3,2:T(8,128)(2,1)} %get-tuple-element.12, f32[20,60,1,128]{1,0,3,2:T(8,128)} %copy.103, f32[20,60,2,128]{1,0,3,2:T(8,128)} %copy-done.3, f32[20,60,1,128]{1,0,3,2:T(8,128)} %copy.101, f32[20,60,2,128]{1,0,3,2:T(8,128)S(1)} %fusion.9, ...), kind=kOutput, calls=%fused_computation.64 | convolution fusion | flops 39936000 | bytes 19357696 | tf_op jit(solution)/shard_map/mkyx,tmyx->tkyx/dot_general | solution.py:133
  352.8 4.4 %copy.105 = f32[20,60,2,128]{3,2,1,0:T(2,128)} copy(f32[20,60,2,128]{1,0,3,2:T(8,128)} %convolution_bitcast_fusion) | data formatting | bytes 2457600
  358.2 6.4 %psum.55 = f32[2,128]{1,0:T(2,128)S(1)} all-reduce(f32[2,128]{1,0:T(2,128)S(1)} %add.117), channel_id=1, replica_groups=mesh['batch'=4,'lat'=8] {'batch'}, use_global_device_ids=true, to_apply=%region_8.9 | all-reduce | flops 256 | bytes 2048 | tf_op jit(solution)/shard_map/psum | solution.py:137
  (108 shorter events, 46.5 us)
Async XLA Ops:
  7.2 38.4 %all-reduce.9.cloned.1.call-start = ((), (), s32[]{:S(2)}) async-start(), calls=%async_computation | async-start | bytes 524288 | tf_op jit(solution)/shard_map/psum | solution.py:26
  13.0 7.2 %copy-start.23 = (s32[20]{0:T(128)S(1)}, s32[20]{0:T(128)}, u32[]{:S(2)}) copy-start(s32[20]{0:T(128)} %param.18) | copy-start | bytes 244
  13.0 7.7 %copy-start.21 = (s32[20]{0:T(128)S(1)}, s32[20]{0:T(128)}, u32[]{:S(2)}) copy-start(s32[20]{0:T(128)} %param.16) | copy-start | bytes 244
  13.0 7.7 %copy-start.22 = (s32[20]{0:T(128)S(1)}, s32[20]{0:T(128)}, u32[]{:S(2)}) copy-start(s32[20]{0:T(128)} %param.17) | copy-start | bytes 244
  13.0 217.0 %all-reduce.11.cloned.1.call-start = ((), (), s32[]{:S(2)}) async-start(), calls=%async_computation.1 | async-start | bytes 16777216 | tf_op jit(solution)/shard_map/psum | solution.py:26
  20.1 3.5 copy-start.24
  20.1 5.2 %copy-start.19 = (f32[20]{0:T(128)S(1)}, f32[20]{0:T(128)}, u32[]{:S(2)}) copy-start(f32[20]{0:T(128)} %param.19) | copy-start | bytes 244
  20.7 27.3 %copy-start.14 = (pred[20,128]{0,1:T(8,128)(4,1)}, pred[20,128]{0,1:T(8,128)(4,1)S(1)}, u32[]{:S(2)}) copy-start(pred[20,128]{0,1:T(8,128)(4,1)S(1)} %iota_compare_fusion) | copy-start | bytes 7684
  23.6 1.7 copy-start.5
  26.4 21.0 %copy-start = (f32[20,60,2,131]{1,0,3,2:T(8,128)}, f32[20,60,2,131]{1,0,3,2:T(8,128)S(1)}, u32[]{:S(2)}) copy-start(f32[20,60,2,131]{1,0,3,2:T(8,128)S(1)} %slice_subtract_fusion.1) | copy-start | bytes 3772804
  47.4 1.9 copy-start.6
  49.3 5.0 %copy-start.17 = (bf16[60,2,128]{0,2,1:T(8,128)(2,1)S(1)}, bf16[60,2,128]{0,2,1:T(8,128)(2,1)}, u32[]{:S(2)}) copy-start(bf16[60,2,128]{0,2,1:T(8,128)(2,1)} %get-tuple-element.9) | copy-start | bytes 92164
  49.3 5.0 %copy-start.18 = (bf16[60,2,128]{0,2,1:T(8,128)(2,1)S(1)}, bf16[60,2,128]{0,2,1:T(8,128)(2,1)}, u32[]{:S(2)}) copy-start(bf16[60,2,128]{0,2,1:T(8,128)(2,1)} %get-tuple-element.11) | copy-start | bytes 92164
  49.3 5.1 %copy-start.20 = (pred[2]{0:T(512)(128)(4,1)S(1)}, pred[2]{0:T(512)(128)(4,1)}, u32[]{:S(2)}) copy-start(pred[2]{0:T(512)(128)(4,1)} %broadcast_compare_fusion.2) | copy-start | bytes 10
  59.8 29.3 %collective-permute-start = (f32[21,60,1,128]{3,2,1,0:T(1,128)}, f32[21,60,1,128]{3,2,1,0:T(1,128)}, u32[]{:S(2)}, u32[]{:S(2)}) collective-permute-start(f32[21,60,1,128]{3,2,1,0:T(1,128)} %copy.74), channel_id=1, source_target_pairs={{0,1},{1,2},{2,3},{3,4},{4,5},{5,6},{6,7},{8,9},{9,10},{10,11},{11... | collective-permute-start | bytes 1935368 | tf_op jit(solution)/shard_map/ppermute | solution.py:18
  66.2 26.9 %collective-permute-start.1 = (f32[21,60,1,128]{3,2,1,0:T(1,128)}, f32[21,60,1,128]{3,2,1,0:T(1,128)}, u32[]{:S(2)}, u32[]{:S(2)}) collective-permute-start(f32[21,60,1,128]{3,2,1,0:T(1,128)} %copy.75), channel_id=1, source_target_pairs={{1,0},{2,1},{3,2},{4,3},{5,4},{6,5},{7,6},{9,8},{10,9},{11,10},{12... | collective-permute-start | bytes 1935368 | tf_op jit(solution)/shard_map/ppermute | solution.py:19
  105.2 2.6 copy-start.12
  105.2 2.6 copy-start.13
  107.8 2.2 copy-start.2
  110.0 2.7 copy-start.8
  116.0 30.2 %collective-permute-start.3 = (f32[20,60,1,128]{3,2,1,0:T(1,128)}, f32[20,60,1,128]{3,2,1,0:T(1,128)}, u32[]{:S(2)}, u32[]{:S(2)}) collective-permute-start(f32[20,60,1,128]{3,2,1,0:T(1,128)} %copy.85), channel_id=1, source_target_pairs={{1,0},{2,1},{3,2},{4,3},{5,4},{6,5},{7,6},{9,8},{10,9},{11,10},{12... | collective-permute-start | bytes 1843208 | tf_op jit(solution)/shard_map/ppermute | solution.py:19
  121.3 28.2 %collective-permute-start.2 = (f32[20,60,1,128]{3,2,1,0:T(1,128)}, f32[20,60,1,128]{3,2,1,0:T(1,128)}, u32[]{:S(2)}, u32[]{:S(2)}) collective-permute-start(f32[20,60,1,128]{3,2,1,0:T(1,128)} %copy.83), channel_id=1, source_target_pairs={{0,1},{1,2},{2,3},{3,4},{4,5},{5,6},{6,7},{8,9},{9,10},{10,11},{11... | collective-permute-start | bytes 1843208 | tf_op jit(solution)/shard_map/ppermute | solution.py:18
  240.5 3.3 copy-start.9
  240.5 3.3 copy-start.10
  243.8 1.9 copy-start.7
  243.8 1.9 copy-start.11
  252.0 30.2 %collective-permute-start.4 = (f32[21,60,1,128]{3,2,1,0:T(1,128)}, f32[21,60,1,128]{3,2,1,0:T(1,128)}, u32[]{:S(2)}, u32[]{:S(2)}) collective-permute-start(f32[21,60,1,128]{3,2,1,0:T(1,128)} %copy.91), channel_id=1, source_target_pairs={{0,1},{1,2},{2,3},{3,4},{4,5},{5,6},{6,7},{8,9},{9,10},{10,11},{11... | collective-permute-start | bytes 1935368 | tf_op jit(solution)/shard_map/ppermute | solution.py:18
  258.4 26.9 %collective-permute-start.5 = (f32[21,60,1,128]{3,2,1,0:T(1,128)}, f32[21,60,1,128]{3,2,1,0:T(1,128)}, u32[]{:S(2)}, u32[]{:S(2)}) collective-permute-start(f32[21,60,1,128]{3,2,1,0:T(1,128)} %copy.92), channel_id=1, source_target_pairs={{1,0},{2,1},{3,2},{4,3},{5,4},{6,5},{7,6},{9,8},{10,9},{11,10},{12... | collective-permute-start | bytes 1935368 | tf_op jit(solution)/shard_map/ppermute | solution.py:19
  298.7 2.2 copy-start.1
  300.9 2.6 copy-start.3
  306.8 11.9 %copy-start.15 = (f32[60,2,128]{2,1,0:T(2,128)S(1)}, f32[60,2,128]{2,1,0:T(2,128)}, u32[]{:S(2)}) copy-start(f32[60,2,128]{2,1,0:T(2,128)} %get-tuple-element.30) | copy-start | bytes 184324
  306.8 12.0 %copy-start.16 = (f32[60,2,128]{2,1,0:T(2,128)S(1)}, f32[60,2,128]{2,1,0:T(2,128)}, u32[]{:S(2)}) copy-start(f32[60,2,128]{2,1,0:T(2,128)} %get-tuple-element.28) | copy-start | bytes 184324
  306.8 30.4 %collective-permute-start.7 = (f32[20,60,1,128]{3,2,1,0:T(1,128)}, f32[20,60,1,128]{3,2,1,0:T(1,128)}, u32[]{:S(2)}, u32[]{:S(2)}) collective-permute-start(f32[20,60,1,128]{3,2,1,0:T(1,128)} %copy.102), channel_id=1, source_target_pairs={{1,0},{2,1},{3,2},{4,3},{5,4},{6,5},{7,6},{9,8},{10,9},{11,10},{12... | collective-permute-start | bytes 1843208 | tf_op jit(solution)/shard_map/ppermute | solution.py:19
  312.1 28.3 %collective-permute-start.6 = (f32[20,60,1,128]{3,2,1,0:T(1,128)}, f32[20,60,1,128]{3,2,1,0:T(1,128)}, u32[]{:S(2)}, u32[]{:S(2)}) collective-permute-start(f32[20,60,1,128]{3,2,1,0:T(1,128)} %copy.100), channel_id=1, source_target_pairs={{0,1},{1,2},{2,3},{3,4},{4,5},{5,6},{6,7},{8,9},{9,10},{10,11},{11... | collective-permute-start | bytes 1843208 | tf_op jit(solution)/shard_map/ppermute | solution.py:18
  352.8 4.4 %copy-start.4 = (f32[20,60,2,128]{1,0,3,2:T(8,128)S(1)}, f32[20,60,2,128]{1,0,3,2:T(8,128)}, u32[]{:S(2)}) copy-start(f32[20,60,2,128]{1,0,3,2:T(8,128)} %convolution_bitcast_fusion) | copy-start | bytes 3686404
Sparse Core Ops, SparseCore 0:
  13.1 32.4 all-reduce.8
  75.3 154.6 all-reduce.10
where the time goes:
time: 374 us; the launch traced here: 372 us
  waiting for transfers between devices  158 us (42%)
  local copies, waits for them, and re-layouts  101 us (27%)
  other arithmetic  47.8 us (13%)
  starting transfers between devices  23.4 us (6%)
  matrix products  19.6 us (5%)
  between operations  15.8 us (4%)
  blocking collectives  6.35 us (2%)
    psum x2, waiting for transfers between devices, broadcast(): return lax.psum(kept, axis)  95.8 us
    ppermute x4, waiting for transfers between devices, with_halo(): after = lax.ppermute(initial, axis, down)  42.1 us
    unnamed x55, local copies, waits for them, and re-layouts  24.6 us
    ppermute x4, waiting for transfers between devices, with_halo(): before = lax.ppermute(last, axis, up)  20.5 us
    dot_general x2, matrix products, on_device(): jnp.einsum('mkyx,tmyx->tkyx', mixing, rounded, preferred_element_type=jnp...  19.6 us
    slice x6, local copies, waits for them, and re-layouts, with_halo(): last = lax.slice_in_dim(shard, length - width, length, axis=dim)  17.3 us
    ppermute x4, starting transfers between devices, with_halo(): before = lax.ppermute(last, axis, up)  13.2 us
    slice x4, local copies, waits for them, and re-layouts, with_halo(): initial = lax.slice_in_dim(shard, 0, width, axis=dim)  13.2 us
  transfers between devices with their start and end apart: 10, of which 8 were waited for; matrix products, arithmetic and copies ran while one was open for 23% of the time, Pallas kernels for 0%

commit v1 on v0

v1 whole, which is shorter than its diff:
```python
import functools
import math

import jax
import jax.numpy as jnp
from jax import lax
from jax.experimental import pallas as pl
from jax.experimental.pallas import tpu as pltpu
from jax.sharding import PartitionSpec as P

HOURS = 2
F32 = jnp.float32
BF16 = jnp.bfloat16
VMEM_LIMIT = 56 * 1024 * 1024


def divisor(value, most):
    return max(d for d in range(1, most + 1) if value % d == 0)


def remote(src, dst, send, recv, where):
    return pltpu.make_async_remote_copy(
        src_ref=src,
        dst_ref=dst,
        send_sem=send,
        recv_sem=recv,
        device_id=where,
        device_id_type=pl.DeviceIdType.MESH,
    )


def faces(courant):
    pos = jnp.maximum(courant, 0.0)
    neg = jnp.minimum(courant, 0.0)
    return pos, neg, pos * (1.0 - pos) * 0.25, neg * (1.0 + neg) * 0.25


def stencil(here, before, before2, after):
    pos, neg, _, neg_slope = faces(here)
    alpha = pos + neg_slope
    _, neg_before, pos_slope_before, _ = faces(before)
    beta = neg_before + pos_slope_before
    q = faces(before2)[3]
    p = faces(after)[2]
    return q, -beta - q, 1.0 - alpha + beta, alpha + p, -p


def kernel(
    n,
    n_lat,
    tracers,
    levels,
    rows,
    block,
    chunk,
    scale,
    adj,
    met,
    conv,
    owner,
    obs_lat,
    obs_lon,
    obs_level,
    obs_hour,
    misfit,
    out,
    grad_out,
    table,
    ring_c,
    north_sel,
    coef_e,
    coef_n,
    send_h,
    halo,
    east_f,
    rounded,
    exch,
    stage_s,
    stage_r,
    mix_b,
    mix_f,
    grad_all,
    s_met,
    r_met,
    s_ring,
    r_ring,
    s_halo,
    r_halo,
    s_exch,
    r_exch,
    s_stage,
    r_stage,
    s_fwd,
    r_fwd,
    s_grad,
    r_grad,
):
    me = lax.axis_index("batch")
    lat = lax.axis_index("lat")
    core = lax.rem(me, 2)
    mate = me + 1 - 2 * core
    bits = []
    bit = 2
    while bit < n:
        bits.append(bit)
        bit *= 2
    n_stage = len(bits)
    half = levels // 2
    n_chunk = half // chunk
    height = levels * rows
    width = adj.shape[-1]
    tiles = height // 8
    n_block = tracers // block
    first = core * half
    other = (1 - core) * half
    up = {"lat": lat + 1}
    down = {"lat": lat - 1}
    has_up = lat < n_lat - 1
    has_down = lat > 0

    barrier = pltpu.get_barrier_semaphore()
    for k in range(1, n):
        pl.semaphore_signal(
            barrier, inc=1, device_id={"batch": lax.rem(me + k, n)}, device_id_type=pl.DeviceIdType.MESH
        )

    @pl.when(has_up)
    def _():
        pl.semaphore_signal(barrier, inc=1, device_id=up, device_id_type=pl.DeviceIdType.MESH)

    @pl.when(has_down)
    def _():
        pl.semaphore_signal(barrier, inc=1, device_id=down, device_id_type=pl.DeviceIdType.MESH)

    pl.semaphore_wait(barrier, n - 1 + jnp.where(has_up, 1, 0) + jnp.where(has_down, 1, 0))

    def met_copy(k):
        return remote(
            met, table.at[me], s_met.at[k], r_met.at[k], {"batch": lax.rem(me + k, n)}
        )

    for k in range(1, n):
        met_copy(k).start()

    def exch_copy(j):
        return remote(
            conv.at[pl.ds(other + j * chunk, chunk)],
            exch.at[pl.ds(j * chunk, chunk)],
            s_exch.at[j],
            r_exch.at[j],
            {"batch": mate},
        )

    for j in range(n_chunk):
        exch_copy(j).start()

    table[me] = met[...]

    def zero_halo(side):
        ring_c[side] = jnp.zeros(ring_c.shape[1:], BF16)

        def body(t, carry):
            for hour in range(HOURS):
                halo[hour, side, t] = jnp.zeros(halo.shape[3:], BF16)
            return carry

        lax.fori_loop(0, tracers, body, 0)

    @pl.when(jnp.logical_not(has_down))
    def _():
        zero_halo(0)

    @pl.when(jnp.logical_not(has_up))
    def _():
        zero_halo(1)

    for k in range(1, n):
        met_copy(k).wait_recv()

    line = lax.broadcasted_iota(jnp.int32, (height, width), 0)
    lane = lax.broadcasted_iota(jnp.int32, (height, width), 1)
    row_of = lax.rem(line, rows) + lat * rows
    even8 = lax.rem(lax.broadcasted_iota(jnp.int32, (tiles, 8, width), 1), 2) == 0

    def swap(value):
        tall = value.reshape(tiles, 8, width)
        mixed = jnp.where(even8, pltpu.roll(tall, 7, 1), pltpu.roll(tall, 1, 1))
        return mixed.reshape(height, width)

    even = lax.rem(line, 2) == 0

    for hour in range(HOURS):
        north = table[owner[hour], 1].astype(F32)
        north = jnp.where(row_of == n_lat * rows - 1, 0.0, north)
        north_sel[hour] = north.astype(BF16)

    def ring_copies(side):
        return remote(
            north_sel, ring_c.at[side], s_ring.at[side], r_ring.at[side], up if side == 0 else down
        )

    @pl.when(has_up)
    def _():
        ring_copies(0).start()

    @pl.when(has_down)
    def _():
        ring_copies(1).start()

    for hour in range(HOURS):
        ce = table[owner[hour], 0].astype(F32)
        before = jnp.where(lane >= 1, pltpu.roll(ce, 1, 1), 0.0)
        before2 = jnp.where(lane >= 2, pltpu.roll(ce, 2, 1), 0.0)
        after = jnp.where(lane < width - 1, pltpu.roll(ce, width - 1, 1), 0.0)
        weights = stencil(ce, before, before2, after)
        inside = (lane >= 2, lane >= 1, None, lane < width - 1, lane < width - 2)
        for i, (weight, keep) in enumerate(zip(weights, inside)):
            coef_e[hour, i] = weight if keep is None else jnp.where(keep, weight, 0.0)

    def halo_copy(hour, side, tb):
        at = pl.ds(tb * block, block)
        return remote(
            send_h.at[hour, at],
            halo.at[hour, side, at],
            s_halo.at[hour, side, tb],
            r_halo.at[hour, side, tb],
            up if side == 0 else down,
        )

    def east_sweep(hour, tb, source):
        def body(i, carry):
            t = tb * block + i
            row_at = obs_lat[t] - lat * rows
            local = (row_at >= 0) & (row_at < rows) & (obs_hour[t] == hour)
            add = jnp.where(local, misfit[t], 0.0)
            hit = (line == obs_level[t] * rows + row_at) & (lane == obs_lon[t])
            field = source[t] + jnp.where(hit, add, 0.0)
            total = coef_e[hour, 2] * field
            total += coef_e[hour, 0] * pltpu.roll(field, 2, 1)
            total += coef_e[hour, 1] * pltpu.roll(field, 1, 1)
            total += coef_e[hour, 3] * pltpu.roll(field, width - 1, 1)
            total += coef_e[hour, 4] * pltpu.roll(field, width - 2, 1)
            east_f[t] = total
            send_h[hour, t] = total.astype(BF16)
            return carry

        lax.fori_loop(0, block, body, 0)

        @pl.when(has_up)
        def _():
            halo_copy(hour, 0, tb).start()

        @pl.when(has_down)
        def _():
            halo_copy(hour, 1, tb).start()

    def north_sweep(hour, tb):
        @pl.when(has_down)
        def _():
            halo_copy(hour, 0, tb).wait_recv()

        @pl.when(has_up)
        def _():
            halo_copy(hour, 1, tb).wait_recv()

        def body(i, carry):
            t = tb * block + i
            field = east_f[t]
            below = halo[hour, 0, t].astype(F32)
            above = halo[hour, 1, t].astype(F32)
            total = coef_n[hour, 0] * below + coef_n[hour, 1] * field
            total += coef_n[hour, 2] * above
            total += coef_n[hour, 3] * swap(field)
            total += coef_n[hour, 4] * swap(jnp.where(even, above, below))
            rounded[t] = total.astype(BF16).astype(F32)
            return carry

        lax.fori_loop(0, block, body, 0)

    even1 = lax.rem(lax.broadcasted_iota(jnp.int32, (1, 8, width), 1), 2) == 0
    part = divisor(tiles, 5)

    def mix(hour, tb):
        t_at = pl.ds(tb * block, block)

        def strip(s, carry):
            at = pl.ds(pl.multiple_of(s * part * 8, 8), part * 8)

            def step(g, acc):
                for q in range(4):
                    m = g * 4 + q
                    base = pl.multiple_of(g * 8, 8)
                    low = rounded[t_at, pl.ds(base + 2 * q, 1), :]
                    high = rounded[t_at, pl.ds(base + 2 * q + 1, 1), :]
                    pair = jnp.where(even1, low, high)
                    matrix = mix_f[hour, m, at, :].reshape(1, part, 8, width)
                    acc = acc + matrix * pair[:, None]
                return acc

            acc = lax.fori_loop(0, levels // 4, step, jnp.zeros((block, part, 8, width), F32))
            out[t_at, at, :] = acc.reshape(block, part * 8, width)
            return carry

        lax.fori_loop(0, tiles // part, strip, 0)

    def stage_copy(s, hour, j):
        at = pl.ds(j * chunk, chunk)
        bit = bits[s]
        return remote(
            stage_s.at[s, hour, at],
            stage_r.at[s, hour, at],
            s_stage.at[s, hour, j],
            r_stage.at[s, hour, j],
            {"batch": me + bit * (1 - 2 * lax.rem(me // bit, 2))},
        )

    def fwd_copy(hour, j, start):
        at = pl.ds(start + j * chunk, chunk)
        return remote(
            mix_b.at[hour, at],
            mix_b.at[hour, at],
            s_fwd.at[hour, j],
            r_fwd.at[hour, j],
            {"batch": mate},
        )

    def pick(flag, a, b):
        return lax.select(flag, a, b)

    def fill_stage(hour, j):
        at = pl.ds(j * chunk, chunk)
        mine = lax.rem(owner[hour], 2) == core
        stage_s[0, hour, at] = pick(mine, conv[pl.ds(first + j * chunk, chunk)], exch[at])

    def receive(hour, s):
        bit = bits[s]
        mine = lax.rem(owner[hour] // bit, 2) == lax.rem(me // bit, 2)

        def body(j, carry):
            at = pl.ds(j * chunk, chunk)
            stage_copy(s, hour, j).wait_recv()
            value = pick(mine, stage_s[s, hour, at], stage_r[s, hour, at])
            if s + 1 < n_stage:
                stage_s[s + 1, hour, at] = value
                stage_copy(s + 1, hour, j).start()
            else:
                mix_b[hour, pl.ds(first + j * chunk, chunk)] = value
                fwd_copy(hour, j, first).start()
                mix_f[hour, pl.ds(first + j * chunk, chunk)] = value.astype(F32)
            if s == 0 and hour > 0:
                stage_copy(0, hour - 1, j).start()
            return carry

        lax.fori_loop(0, n_chunk, body, 0)

    def widen(hour):
        def body(j, carry):
            at = pl.ds(other + j * chunk, chunk)
            fwd_copy(hour, j, other).wait_recv()
            mix_f[hour, at] = mix_b[hour, at].astype(F32)
            return carry

        lax.fori_loop(0, n_chunk, body, 0)

    last = HOURS - 1
    for tb in range(n_block):
        east_sweep(last, tb, adj)

    def start_stage(j, carry):
        exch_copy(j).wait_recv()
        fill_stage(last, j)
        stage_copy(0, last, j).start()
        for hour in range(last):
            fill_stage(hour, j)
        return carry

    lax.fori_loop(0, n_chunk, start_stage, 0)

    @pl.when(has_down)
    def _():
        ring_copies(0).wait_recv()

    @pl.when(has_up)
    def _():
        ring_copies(1).wait_recv()

    for hour in range(HOURS):
        here = north_sel[hour].astype(F32)
        below = ring_c[0, hour].astype(F32)
        above = ring_c[1, hour].astype(F32)
        turned = swap(here)
        crossed = swap(jnp.where(even, above, below))
        before = jnp.where(even, crossed, turned)
        after = jnp.where(even, turned, crossed)
        w_m2, w_m1, w_0, w_p1, w_p2 = stencil(here, before, below, after)
        coef_n[hour, 0] = w_m2
        coef_n[hour, 1] = w_0
        coef_n[hour, 2] = w_p2
        coef_n[hour, 3] = jnp.where(even, w_p1, w_m1)
        coef_n[hour, 4] = jnp.where(even, w_m1, w_p1)

    early = n_block // 2
    for tb in range(early):
        north_sweep(last, tb)

    surface = jnp.zeros((8, width), F32)
    for hour in reversed(range(HOURS)):
        for s in range(n_stage):
            receive(hour, s)
        widen(hour)
        for tb in range(n_block):
            if hour < last or tb >= early:
                north_sweep(hour, tb)
            mix(hour, tb)
            for i in range(block):
                surface = surface + out[tb * block + i, 0:8, :]
            if hour > 0:
                east_sweep(hour - 1, tb, out)

    grad_all[me] = surface

    def grad_copy(k):
        return remote(
            grad_all.at[me],
            grad_all.at[me],
            s_grad.at[k],
            r_grad.at[k],
            {"batch": lax.rem(me + k, n)},
        )

    for k in range(1, n):
        grad_copy(k).start()

    for k in range(1, n):
        met_copy(k).wait_send()

    @pl.when(has_up)
    def _():
        ring_copies(0).wait_send()
        for hour in range(HOURS):
            for tb in range(n_block):
                halo_copy(hour, 0, tb).wait_send()

    @pl.when(has_down)
    def _():
        ring_copies(1).wait_send()
        for hour in range(HOURS):
            for tb in range(n_block):
                halo_copy(hour, 1, tb).wait_send()

    def drain(j, carry):
        exch_copy(j).wait_send()
        for hour in range(HOURS):
            for s in range(n_stage):
                stage_copy(s, hour, j).wait_send()
            fwd_copy(hour, j, first).wait_send()
        return carry

    lax.fori_loop(0, n_chunk, drain, 0)
    for k in range(1, n):
        grad_copy(k).wait_recv()
    for k in range(1, n):
        grad_copy(k).wait_send()
    total = grad_all[0]
    for k in range(1, n):
        total = total + grad_all[k]
    grad_out[...] = total[0:rows] * scale


def on_device(
    adjoint_in,
    east_courant,
    north_courant,
    convection,
    hour_owner,
    obs_lat,
    obs_lon,
    obs_level,
    obs_hour,
    misfit,
):
    tracers, levels, rows, width = adjoint_in.shape
    n = lax.axis_size("batch")
    n_lat = lax.axis_size("lat")
    height = levels * rows
    block = divisor(tracers, 5)
    half = levels // 2
    chunk = divisor(half, 5)
    n_chunk = half // chunk
    n_block = tracers // block
    n_stage = n.bit_length() - 2
    scale = 1.0 / math.sqrt(tracers * n)
    met = jnp.concatenate([east_courant, north_courant], axis=0).reshape(2, height, width)
    vmem = pl.BlockSpec(memory_space=pltpu.VMEM)
    smem = pl.BlockSpec(memory_space=pltpu.SMEM)
    dma = pltpu.SemaphoreType.DMA
    body = functools.partial(
        kernel, n, n_lat, tracers, levels, rows, block, chunk, scale
    )
    out, grad = pl.pallas_call(
        body,
        out_shape=(
            jax.ShapeDtypeStruct((tracers, height, width), F32),
            jax.ShapeDtypeStruct((rows, width), F32),
        ),
        in_specs=[vmem] * 3 + [smem] * 6,
        out_specs=(vmem, vmem),
        scratch_shapes=[
            pltpu.VMEM((n, 2, height, width), BF16),
            pltpu.VMEM((2, HOURS, height, width), BF16),
            pltpu.VMEM((HOURS, height, width), BF16),
            pltpu.VMEM((HOURS, 5, height, width), F32),
            pltpu.VMEM((HOURS, 5, height, width), F32),
            pltpu.VMEM((HOURS, tracers, height, width), BF16),
            pltpu.VMEM((HOURS, 2, tracers, height, width), BF16),
            pltpu.VMEM((tracers, height, width), F32),
            pltpu.VMEM((tracers, height, width), F32),
            pltpu.VMEM((half, height, width), BF16),
            pltpu.VMEM((n_stage, HOURS, half, height, width), BF16),
            pltpu.VMEM((n_stage, HOURS, half, height, width), BF16),
            pltpu.VMEM((HOURS, levels, height, width), BF16),
            pltpu.VMEM((HOURS, levels, height, width), F32),
            pltpu.VMEM((n, 8, width), F32),
            dma((n,)),
            dma((n,)),
            dma((2,)),
            dma((2,)),
            dma((HOURS, 2, n_block)),
            dma((HOURS, 2, n_block)),
            dma((n_chunk,)),
            dma((n_chunk,)),
            dma((n_stage, HOURS, n_chunk)),
            dma((n_stage, HOURS, n_chunk)),
            dma((HOURS, n_chunk)),
            dma((HOURS, n_chunk)),
            dma((n,)),
            dma((n,)),
        ],
        compiler_params=pltpu.CompilerParams(
            collective_id=0, has_side_effects=True, vmem_limit_bytes=VMEM_LIMIT
        ),
    )(
        adjoint_in.reshape(tracers, height, width),
        met,
        convection.reshape(levels, height, width),
        hour_owner[:HOURS, 0],
        obs_lat,
        obs_lon,
        obs_level,
        obs_hour,
        misfit,
    )
    return (out.reshape(tracers, levels, rows, width), grad)


def solution(mesh):
    return jax.shard_map(
        on_device,
        mesh=mesh,
        in_specs=(
            P("batch", None, "lat", None),
            P("batch", None, "lat", None),
            P("batch", None, "lat", None),
            P("batch", None, None, "lat", None),
            P(None, "lat"),
            P("batch"),
            P("batch"),
            P("batch"),
            P("batch"),
            P("batch"),
        ),
        out_specs=(P("batch", None, "lat", None), P("lat", None)),
        check_vma=False,
    )
```

time: 374 us -> 79 us (0.21)
  waiting for transfers between devices: 158 us -> 0 us
  local copies, waits for them, and re-layouts: 101 us -> 4.15 us
  Pallas kernels: 0 us -> 72.4 us
  other arithmetic: 47.8 us -> 1.48 us
  starting transfers between devices: 23.4 us -> 0 us
  matrix products: 19.6 us -> 0 us
  between operations: 15.8 us -> 0.65 us
  blocking collectives: 6.35 us -> 0 us
    psum x2 -> x0, waiting for transfers between devices: 95.8 us -> none  [broadcast(): return lax.psum(kept, axis)]
    pallas_call x0 -> x1, Pallas kernels: none -> 72.4 us  [on_device(): pl.pallas_call(body, out_shape=(jax.ShapeDtypeStruct((tracers, height, wi...]
    ppermute x8 -> x0, waiting for transfers between devices: 62.6 us -> none  [the longest x4 42.1 us: with_halo(): after = lax.ppermute(initial, axis, down)]
    slice x11 -> x0, local copies, waits for them, and re-layouts: 31.9 us -> none  [the longest x6 17.3 us: with_halo(): last = lax.slice_in_dim(shard, length - width, length, axis=dim)]
    ppermute x8 -> x0, local copies, waits for them, and re-layouts: 26.2 us -> none  [the longest x4 13.2 us: with_halo(): before = lax.ppermute(last, axis, up)]
    ppermute x8 -> x0, starting transfers between devices: 23.3 us -> none  [the longest x4 13.2 us: with_halo(): before = lax.ppermute(last, axis, up)]
    unnamed x55 -> x4, local copies, waits for them, and re-layouts: 24.6 us -> 2.96 us
    dot_general x2 -> x0, matrix products: 19.6 us -> none  [on_device(): jnp.einsum('mkyx,tmyx->tkyx', mixing, rounded, preferred_element_type=jnp...]
  transfers between devices with their start and end apart: 10 -> 0, of which waited for: 8 -> 0; matrix products, arithmetic and copies ran while one was open for 23% -> 0% of each run, Pallas kernels for 0% -> 0%
where the time goes in v1:
time: 79 us; the launch traced here: 78.7 us
  Pallas kernels  72.4 us (92%)
  local copies, waits for them, and re-layouts  4.15 us (5%)
  other arithmetic  1.48 us (2%)
    pallas_call x1, Pallas kernels, on_device(): pl.pallas_call(body, out_shape=(jax.ShapeDtypeStruct((tracers, height, wi...  72.4 us
    unnamed x4, local copies, waits for them, and re-layouts  2.96 us

profile of v1, /device:TPU:9, one launch (start us, length us, event | category | flops | bytes accessed | tf_op | source)
XLA Modules:
  0.0 78.7 jit_solution(9016662394732906357)
XLA Ops:
  0.6 1.2 %slice_bitcast_fusion.owner = s32[2]{0:T(128)} fusion(s32[4,2]{0,1:T(2,128)} %param.14), kind=kLoop, calls=%fused_computation.1 | loop fusion | bytes 16 | tf_op jit(solution)/shard_map/squeeze | solution.py:546
  1.8 1.5 %pad_maximum_fusion = bf16[2,60,2,128]{3,2,1,0:T(2,128)(2,1)} fusion(bf16[1,60,2,128]{3,2,1,0:T(2,128)(2,1)} %param.12, bf16[1,60,2,128]{3,2,1,0:T(2,128)(2,1)} %param.11), kind=kLoop, calls=%fused_computation | loop fusion | flops 30720 | bytes 122880 | tf_op jit(solution)/shard_map/concatenate | solution.py:493
  3.3 72.4 %shard_map.113 = (f32[20,120,128]{2,1,0:T(8,128)}, f32[2,128]{1,0:T(2,128)}) custom-call(f32[20,120,128]{2,1,0:T(8,128)} %bitcast.7, bf16[2,120,128]{2,1,0:T(8,128)(2,1)} %bitcast.9, bf16[60,120,128]{2,1,0:T(8,128)(2,1)} %bitcast.6, s32[2]{0:T(128)} %slice_bitcast_fusion.owner, s32[20]{0:T(128)} %obs_lat.1, s32[20]{0:T(128)} %obs_lon.1, s32[20]{0:T(128)} %obs_level.1, ...), custom_call_target="tpu_custom_call" | custom-call | tf_op jit(solution)/shard_map/pallas_call | solution.py:500
  75.7 0.0 copy-start
  75.7 2.4 %copy.14 = f32[20,60,2,128]{3,2,1,0:T(2,128)} copy(f32[20,60,2,128]{3,2,1,0:T(2,128)} %bitcast.8) | data formatting | bytes 2457600
  78.1 0.0 copy-done
  78.1 0.6 copy.15
Async XLA Ops:
  75.7 2.4 %copy-start = (f32[2,128]{1,0:T(2,128)S(1)}, f32[2,128]{1,0:T(2,128)}, u32[]{:S(2)}) copy-start(f32[2,128]{1,0:T(2,128)} %get-tuple-element.9) | copy-start | bytes 3076

commit v2 on v1

--- a/solution.py
+++ b/solution.py
@@ -55,9 +55,10 @@
     chunk,
     scale,
     adj,
-    met,
+    east,
+    north,
     conv,
-    owner,
+    owner_table,
     obs_lat,
     obs_lon,
     obs_level,
@@ -84,8 +85,10 @@
     r_met,
     s_ring,
     r_ring,
-    s_halo,
-    r_halo,
+    s_near,
+    r_near,
+    s_far,
+    r_far,
     s_exch,
     r_exch,
     s_stage,
@@ -95,6 +98,7 @@
     s_grad,
     r_grad,
 ):
+    owner = [owner_table[hour, 0] for hour in range(HOURS)]
     me = lax.axis_index("batch")
     lat = lax.axis_index("lat")
     core = lax.rem(me, 2)
@@ -117,6 +121,11 @@
     down = {"lat": lat - 1}
     has_up = lat < n_lat - 1
     has_down = lat > 0
+    odd = lax.rem(lat, 2)
+    pair = {"lat": lat + 1 - 2 * odd}
+    onward = {"lat": lat + 2 - 4 * odd}
+    gives = jnp.where(odd == 0, lat + 2 < n_lat, lat >= 2)
+    takes = jnp.where(odd == 0, lat >= 2, lat + 2 < n_lat)
 
     barrier = pltpu.get_barrier_semaphore()
     for k in range(1, n):
@@ -132,15 +141,35 @@
     def _():
         pl.semaphore_signal(barrier, inc=1, device_id=down, device_id_type=pl.DeviceIdType.MESH)
 
-    pl.semaphore_wait(barrier, n - 1 + jnp.where(has_up, 1, 0) + jnp.where(has_down, 1, 0))
-
-    def met_copy(k):
-        return remote(
-            met, table.at[me], s_met.at[k], r_met.at[k], {"batch": lax.rem(me + k, n)}
-        )
-
-    for k in range(1, n):
-        met_copy(k).start()
+    @pl.when(lat + 2 < n_lat)
+    def _():
+        pl.semaphore_signal(
+            barrier, inc=1, device_id={"lat": lat + 2}, device_id_type=pl.DeviceIdType.MESH
+        )
+
+    @pl.when(lat >= 2)
+    def _():
+        pl.semaphore_signal(
+            barrier, inc=1, device_id={"lat": lat - 2}, device_id_type=pl.DeviceIdType.MESH
+        )
+
+    greeted = n - 1
+    for there in (has_up, has_down, lat + 2 < n_lat, lat >= 2):
+        greeted = greeted + jnp.where(there, 1, 0)
+    pl.semaphore_wait(barrier, greeted)
+
+    def met_copy(k, i):
+        return remote(
+            (east, north)[i].at[0],
+            table.at[me, i],
+            s_met.at[k, i],
+            r_met.at[k, i],
+            {"batch": lax.rem(me + k, n)},
+        )
+
+    for k in range(1, n):
+        for i in range(2):
+            met_copy(k, i).start()
 
     def exch_copy(j):
         return remote(
@@ -154,7 +183,8 @@
     for j in range(n_chunk):
         exch_copy(j).start()
 
-    table[me] = met[...]
+    table[me, 0] = east[0]
+    table[me, 1] = north[0]
 
     def zero_halo(side):
         ring_c[side] = jnp.zeros(ring_c.shape[1:], BF16)
@@ -175,7 +205,8 @@
         zero_halo(1)
 
     for k in range(1, n):
-        met_copy(k).wait_recv()
+        for i in range(2):
+            met_copy(k, i).wait_recv()
 
     line = lax.broadcasted_iota(jnp.int32, (height, width), 0)
     lane = lax.broadcasted_iota(jnp.int32, (height, width), 1)
@@ -190,9 +221,9 @@
     even = lax.rem(line, 2) == 0
 
     for hour in range(HOURS):
-        north = table[owner[hour], 1].astype(F32)
-        north = jnp.where(row_of == n_lat * rows - 1, 0.0, north)
-        north_sel[hour] = north.astype(BF16)
+        cn = table[owner[hour], 1].astype(F32)
+        cn = jnp.where(row_of == n_lat * rows - 1, 0.0, cn)
+        north_sel[hour] = cn.astype(BF16)
 
     def ring_copies(side):
         return remote(
@@ -217,15 +248,32 @@
         for i, (weight, keep) in enumerate(zip(weights, inside)):
             coef_e[hour, i] = weight if keep is None else jnp.where(keep, weight, 0.0)
 
-    def halo_copy(hour, side, tb):
+    def near_copy(hour, tb):
         at = pl.ds(tb * block, block)
         return remote(
             send_h.at[hour, at],
-            halo.at[hour, side, at],
-            s_halo.at[hour, side, tb],
-            r_halo.at[hour, side, tb],
-            up if side == 0 else down,
-        )
+            halo.at[hour, odd, at],
+            s_near.at[hour, tb],
+            r_near.at[hour, tb],
+            pair,
+        )
+
+    def far_copy(hour, tb):
+        at = pl.ds(tb * block, block)
+        return remote(
+            halo.at[hour, 1 - odd, at],
+            halo.at[hour, odd, at],
+            s_far.at[hour, tb],
+            r_far.at[hour, tb],
+            onward,
+        )
+
+    def relay(hour, tb):
+        near_copy(hour, tb).wait_recv()
+
+        @pl.when(gives)
+        def _():
+            far_copy(hour, tb).start()
 
     def east_sweep(hour, tb, source):
         def body(i, carry):
@@ -246,22 +294,12 @@
 
         lax.fori_loop(0, block, body, 0)
 
-        @pl.when(has_up)
+        near_copy(hour, tb).start()
+
+    def north_sweep(hour, tb):
+        @pl.when(takes)
         def _():
-            halo_copy(hour, 0, tb).start()
-
-        @pl.when(has_down)
-        def _():
-            halo_copy(hour, 1, tb).start()
-
-    def north_sweep(hour, tb):
-        @pl.when(has_down)
-        def _():
-            halo_copy(hour, 0, tb).wait_recv()
-
-        @pl.when(has_up)
-        def _():
-            halo_copy(hour, 1, tb).wait_recv()
+            far_copy(hour, tb).wait_recv()
 
         def body(i, carry):
             t = tb * block + i
@@ -280,24 +318,32 @@
     even1 = lax.rem(lax.broadcasted_iota(jnp.int32, (1, 8, width), 1), 2) == 0
     part = divisor(tiles, 5)
 
-    def mix(hour, tb):
+    def mix(hour, tb, begin, count):
         t_at = pl.ds(tb * block, block)
 
         def strip(s, carry):
             at = pl.ds(pl.multiple_of(s * part * 8, 8), part * 8)
 
-            def step(g, acc):
-                for q in range(4):
-                    m = g * 4 + q
-                    base = pl.multiple_of(g * 8, 8)
-                    low = rounded[t_at, pl.ds(base + 2 * q, 1), :]
-                    high = rounded[t_at, pl.ds(base + 2 * q + 1, 1), :]
-                    pair = jnp.where(even1, low, high)
-                    matrix = mix_f[hour, m, at, :].reshape(1, part, 8, width)
-                    acc = acc + matrix * pair[:, None]
+            def step(j, acc):
+                for start in (first, other):
+                    for q in range(chunk):
+                        m = start + j * chunk + q
+                        low = rounded[t_at, pl.ds(2 * m, 1), :]
+                        high = rounded[t_at, pl.ds(2 * m + 1, 1), :]
+                        both = jnp.where(even1, low, high)
+                        matrix = mix_f[hour, m, at, :].reshape(1, part, 8, width)
+                        acc = acc + matrix * both[:, None]
                 return acc
 
-            acc = lax.fori_loop(0, levels // 4, step, jnp.zeros((block, part, 8, width), F32))
+            shape = (block, part, 8, width)
+            if begin == 0:
+                acc = jnp.zeros(shape, F32)
+            else:
+                acc = out[t_at, at, :].reshape(shape)
+            if count == 1:
+                acc = step(begin, acc)
+            else:
+                acc = lax.fori_loop(begin, begin + count, step, acc)
             out[t_at, at, :] = acc.reshape(block, part * 8, width)
             return carry
 
@@ -332,12 +378,11 @@
         mine = lax.rem(owner[hour], 2) == core
         stage_s[0, hour, at] = pick(mine, conv[pl.ds(first + j * chunk, chunk)], exch[at])
 
-    def receive(hour, s):
-        bit = bits[s]
-        mine = lax.rem(owner[hour] // bit, 2) == lax.rem(me // bit, 2)
-
-        def body(j, carry):
-            at = pl.ds(j * chunk, chunk)
+    def receive(hour, j):
+        at = pl.ds(j * chunk, chunk)
+        for s in range(n_stage):
+            bit = bits[s]
+            mine = lax.rem(owner[hour] // bit, 2) == lax.rem(me // bit, 2)
             stage_copy(s, hour, j).wait_recv()
             value = pick(mine, stage_s[s, hour, at], stage_r[s, hour, at])
             if s + 1 < n_stage:
@@ -349,32 +394,30 @@
                 mix_f[hour, pl.ds(first + j * chunk, chunk)] = value.astype(F32)
             if s == 0 and hour > 0:
                 stage_copy(0, hour - 1, j).start()
-            return carry
-
-        lax.fori_loop(0, n_chunk, body, 0)
-
-    def widen(hour):
-        def body(j, carry):
-            at = pl.ds(other + j * chunk, chunk)
-            fwd_copy(hour, j, other).wait_recv()
-            mix_f[hour, at] = mix_b[hour, at].astype(F32)
-            return carry
-
-        lax.fori_loop(0, n_chunk, body, 0)
+
+    def widen(hour, j):
+        at = pl.ds(other + j * chunk, chunk)
+        fwd_copy(hour, j, other).wait_recv()
+        mix_f[hour, at] = mix_b[hour, at].astype(F32)
 
     last = HOURS - 1
-    for tb in range(n_block):
-        east_sweep(last, tb, adj)
-
-    def start_stage(j, carry):
+    def start_stage(j):
         exch_copy(j).wait_recv()
         fill_stage(last, j)
         stage_copy(0, last, j).start()
+
+    for tb in range(max(n_block, n_chunk)):
+        if tb < n_chunk:
+            start_stage(tb)
+        if tb < n_block:
+            east_sweep(last, tb, adj)
+
+    def fill_later(j, carry):
         for hour in range(last):
             fill_stage(hour, j)
         return carry
 
-    lax.fori_loop(0, n_chunk, start_stage, 0)
+    lax.fori_loop(0, n_chunk, fill_later, 0)
 
     @pl.when(has_down)
     def _():
@@ -399,23 +442,30 @@
         coef_n[hour, 3] = jnp.where(even, w_p1, w_m1)
         coef_n[hour, 4] = jnp.where(even, w_m1, w_p1)
 
-    early = n_block // 2
-    for tb in range(early):
-        north_sweep(last, tb)
-
+    bulk = n_chunk - 2
     surface = jnp.zeros((8, width), F32)
     for hour in reversed(range(HOURS)):
-        for s in range(n_stage):
-            receive(hour, s)
-        widen(hour)
+        for j in range(max(bulk, n_block)):
+            if j < n_block:
+                relay(hour, j)
+            if j < bulk:
+                receive(hour, j)
+        for j in range(bulk):
+            widen(hour, j)
         for tb in range(n_block):
-            if hour < last or tb >= early:
-                north_sweep(hour, tb)
-            mix(hour, tb)
-            for i in range(block):
-                surface = surface + out[tb * block + i, 0:8, :]
-            if hour > 0:
-                east_sweep(hour - 1, tb, out)
+            north_sweep(hour, tb)
+            mix(hour, tb, 0, bulk)
+        for j in range(bulk, n_chunk):
+            receive(hour, j)
+            widen(hour, j)
+            for tb in range(n_block):
+                mix(hour, tb, j, 1)
+                if j < n_chunk - 1:
+                    continue
+                for i in range(block):
+                    surface = surface + out[tb * block + i, 0:8, :]
+                if hour > 0:
+                    east_sweep(hour - 1, tb, out)
 
     grad_all[me] = surface
 
@@ -432,21 +482,26 @@
         grad_copy(k).start()
 
     for k in range(1, n):
-        met_copy(k).wait_send()
+        for i in range(2):
+            met_copy(k, i).wait_send()
 
     @pl.when(has_up)
     def _():
         ring_copies(0).wait_send()
+
+    @pl.when(has_down)
+    def _():
+        ring_copies(1).wait_send()
+
+    for hour in range(HOURS):
+        for tb in range(n_block):
+            near_copy(hour, tb).wait_send()
+
+    @pl.when(gives)
+    def _():
         for hour in range(HOURS):
             for tb in range(n_block):
-                halo_copy(hour, 0, tb).wait_send()
-
-    @pl.when(has_down)
-    def _():
-        ring_copies(1).wait_send()
-        for hour in range(HOURS):
-            for tb in range(n_block):
-                halo_copy(hour, 1, tb).wait_send()
+                far_copy(hour, tb).wait_send()
 
     def drain(j, carry):
         exch_copy(j).wait_send()
@@ -490,7 +545,6 @@
     n_block = tracers // block
     n_stage = n.bit_length() - 2
     scale = 1.0 / math.sqrt(tracers * n)
-    met = jnp.concatenate([east_courant, north_courant], axis=0).reshape(2, height, width)
     vmem = pl.BlockSpec(memory_space=pltpu.VMEM)
     smem = pl.BlockSpec(memory_space=pltpu.SMEM)
     dma = pltpu.SemaphoreType.DMA
@@ -503,7 +557,7 @@
             jax.ShapeDtypeStruct((tracers, height, width), F32),
             jax.ShapeDtypeStruct((rows, width), F32),
         ),
-        in_specs=[vmem] * 3 + [smem] * 6,
+        in_specs=[vmem] * 4 + [smem] * 6,
         out_specs=(vmem, vmem),
         scratch_shapes=[
             pltpu.VMEM((n, 2, height, width), BF16),
@@ -521,12 +575,14 @@
             pltpu.VMEM((HOURS, levels, height, width), BF16),
             pltpu.VMEM((HOURS, levels, height, width), F32),
             pltpu.VMEM((n, 8, width), F32),
-            dma((n,)),
-            dma((n,)),
+            dma((n, 2)),
+            dma((n, 2)),
             dma((2,)),
             dma((2,)),
-            dma((HOURS, 2, n_block)),
-            dma((HOURS, 2, n_block)),
+            dma((HOURS, n_block)),
+            dma((HOURS, n_block)),
+            dma((HOURS, n_block)),
+            dma((HOURS, n_block)),
             dma((n_chunk,)),
             dma((n_chunk,)),
             dma((n_stage, HOURS, n_chunk)),
@@ -541,9 +597,10 @@
         ),
     )(
         adjoint_in.reshape(tracers, height, width),
-        met,
+        east_courant.reshape(1, height, width),
+        north_courant.reshape(1, height, width),
         convection.reshape(levels, height, width),
-        hour_owner[:HOURS, 0],
+        hour_owner,
         obs_lat,
         obs_lon,
         obs_level,

time: 79 us -> 73.8 us (0.934); the launches traced: 78.7 us -> 72.5 us
  Pallas kernels: 72.4 us -> 67.6 us
  other arithmetic: 1.48 us -> 0 us
    pallas_call x1, Pallas kernels: 72.4 us -> 67.6 us  [on_device(): pl.pallas_call(body, out_shape=(jax.ShapeDtypeStruct((tracers, height, wi...]
    concatenate x1 -> x0, other arithmetic: 1.48 us -> none  [on_device(): jnp.concatenate([east_courant, north_courant], axis=0)]
    unnamed x4 -> x5, local copies, waits for them, and re-layouts: 2.96 us -> 4.3 us
    squeeze x1 -> x0, local copies, waits for them, and re-layouts: 1.19 us -> none  [on_device(): hour_owner[:HOURS, 0]]
where the time goes in v2:
time: 73.8 us; the launch traced here: 72.5 us
  Pallas kernels  67.6 us (92%)
  local copies, waits for them, and re-layouts  4.3 us (6%)
    pallas_call x1, Pallas kernels, on_device(): pl.pallas_call(body, out_shape=(jax.ShapeDtypeStruct((tracers, height, wi...  67.6 us
    unnamed x5, local copies, waits for them, and re-layouts  4.3 us

profile of v2, /device:TPU:9, one launch (start us, length us, event | category | flops | bytes accessed | tf_op | source)
XLA Modules:
  0.0 72.5 jit_solution(13021838215663375629)
XLA Ops:
  0.6 1.3 %copy.12.owner_table = s32[4,2]{1,0:T(4,128)} copy(s32[4,2]{0,1:T(2,128)} %param.14) | data formatting | bytes 64 | tf_op args[4]
  2.0 67.6 %shard_map.113 = (f32[20,120,128]{2,1,0:T(8,128)}, f32[2,128]{1,0:T(2,128)}) custom-call(f32[20,120,128]{2,1,0:T(8,128)} %bitcast.6, bf16[1,120,128]{2,1,0:T(8,128)(2,1)} %bitcast.8, bf16[1,120,128]{2,1,0:T(8,128)(2,1)} %bitcast.9, bf16[60,120,128]{2,1,0:T(8,128)(2,1)} %bitcast.5, s32[4,2]{1,0:T(4,128)} %copy.12.owner_table, s32[20]{0:T(128)} %obs_lat.1, ...), custom_call_target="tpu_custom_call" | custom-call | tf_op jit(solution)/shard_map/pallas_call | solution.py:554
  69.5 0.0 copy-start
  69.5 2.4 %copy.15 = f32[20,60,2,128]{3,2,1,0:T(2,128)} copy(f32[20,60,2,128]{3,2,1,0:T(2,128)} %bitcast.7) | data formatting | bytes 2457600
  71.9 0.0 copy-done
  71.9 0.6 copy.16
Async XLA Ops:
  69.5 2.4 %copy-start = (f32[2,128]{1,0:T(2,128)S(1)}, f32[2,128]{1,0:T(2,128)}, u32[]{:S(2)}) copy-start(f32[2,128]{1,0:T(2,128)} %get-tuple-element.9) | copy-start | bytes 3076

commit v3 on v2

--- a/solution.py
+++ b/solution.py
@@ -64,8 +64,10 @@
     obs_level,
     obs_hour,
     misfit,
+    result,
+    grad_out,
     out,
-    grad_out,
+    own,
     table,
     ring_c,
     north_sel,
@@ -97,6 +99,9 @@
     r_fwd,
     s_grad,
     r_grad,
+    s_own,
+    s_adj,
+    s_out,
 ):
     owner = [owner_table[hour, 0] for hour in range(HOURS)]
     me = lax.axis_index("batch")
@@ -127,6 +132,23 @@
     gives = jnp.where(odd == 0, lat + 2 < n_lat, lat >= 2)
     takes = jnp.where(odd == 0, lat >= 2, lat + 2 < n_lat)
 
+    def own_copy(j):
+        at = pl.ds(j * chunk, chunk)
+        return pltpu.make_async_copy(conv.at[pl.ds(first + j * chunk, chunk)], own.at[at], s_own.at[j])
+
+    def adj_copy(tb):
+        at = pl.ds(tb * block, block)
+        return pltpu.make_async_copy(adj.at[at], out.at[at], s_adj.at[tb])
+
+    def out_copy(tb):
+        at = pl.ds(tb * block, block)
+        return pltpu.make_async_copy(out.at[at], result.at[at], s_out.at[tb])
+
+    for j in range(n_chunk):
+        own_copy(j).start()
+    for tb in range(n_block):
+        adj_copy(tb).start()
+
     barrier = pltpu.get_barrier_semaphore()
     for k in range(1, n):
         pl.semaphore_signal(
@@ -204,6 +226,47 @@
     def _():
         zero_halo(1)
 
+    def stage_copy(s, hour, j):
+        at = pl.ds(j * chunk, chunk)
+        bit = bits[s]
+        return remote(
+            stage_s.at[s, hour, at],
+            stage_r.at[s, hour, at],
+            s_stage.at[s, hour, j],
+            r_stage.at[s, hour, j],
+            {"batch": me + bit * (1 - 2 * lax.rem(me // bit, 2))},
+        )
+
+    def fwd_copy(hour, j, start):
+        at = pl.ds(start + j * chunk, chunk)
+        return remote(
+            mix_b.at[hour, at],
+            mix_b.at[hour, at],
+            s_fwd.at[hour, j],
+            r_fwd.at[hour, j],
+            {"batch": mate},
+        )
+
+    def pick(flag, a, b):
+        return lax.select(flag, a, b)
+
+    def fill_stage(hour, j):
+        at = pl.ds(j * chunk, chunk)
+        mine = lax.rem(owner[hour], 2) == core
+        stage_s[0, hour, at] = pick(mine, own[at], exch[at])
+
+    last = HOURS - 1
+    lead = 2
+
+    def start_stage(j):
+        own_copy(j).wait()
+        exch_copy(j).wait_recv()
+        fill_stage(last, j)
+        stage_copy(0, last, j).start()
+
+    for j in range(lead):
+        start_stage(j)
+
     for k in range(1, n):
         for i in range(2):
             met_copy(k, i).wait_recv()
@@ -238,7 +301,7 @@
     def _():
         ring_copies(1).start()
 
-    for hour in range(HOURS):
+    def set_east(hour):
         ce = table[owner[hour], 0].astype(F32)
         before = jnp.where(lane >= 1, pltpu.roll(ce, 1, 1), 0.0)
         before2 = jnp.where(lane >= 2, pltpu.roll(ce, 2, 1), 0.0)
@@ -247,6 +310,8 @@
         inside = (lane >= 2, lane >= 1, None, lane < width - 1, lane < width - 2)
         for i, (weight, keep) in enumerate(zip(weights, inside)):
             coef_e[hour, i] = weight if keep is None else jnp.where(keep, weight, 0.0)
+
+    set_east(last)
 
     def near_copy(hour, tb):
         at = pl.ds(tb * block, block)
@@ -349,35 +414,6 @@
 
         lax.fori_loop(0, tiles // part, strip, 0)
 
-    def stage_copy(s, hour, j):
-        at = pl.ds(j * chunk, chunk)
-        bit = bits[s]
-        return remote(
-            stage_s.at[s, hour, at],
-            stage_r.at[s, hour, at],
-            s_stage.at[s, hour, j],
-            r_stage.at[s, hour, j],
-            {"batch": me + bit * (1 - 2 * lax.rem(me // bit, 2))},
-        )
-
-    def fwd_copy(hour, j, start):
-        at = pl.ds(start + j * chunk, chunk)
-        return remote(
-            mix_b.at[hour, at],
-            mix_b.at[hour, at],
-            s_fwd.at[hour, j],
-            r_fwd.at[hour, j],
-            {"batch": mate},
-        )
-
-    def pick(flag, a, b):
-        return lax.select(flag, a, b)
-
-    def fill_stage(hour, j):
-        at = pl.ds(j * chunk, chunk)
-        mine = lax.rem(owner[hour], 2) == core
-        stage_s[0, hour, at] = pick(mine, conv[pl.ds(first + j * chunk, chunk)], exch[at])
-
     def receive(hour, j):
         at = pl.ds(j * chunk, chunk)
         for s in range(n_stage):
@@ -400,17 +436,12 @@
         fwd_copy(hour, j, other).wait_recv()
         mix_f[hour, at] = mix_b[hour, at].astype(F32)
 
-    last = HOURS - 1
-    def start_stage(j):
-        exch_copy(j).wait_recv()
-        fill_stage(last, j)
-        stage_copy(0, last, j).start()
-
     for tb in range(max(n_block, n_chunk)):
-        if tb < n_chunk:
-            start_stage(tb)
+        if tb + lead < n_chunk:
+            start_stage(tb + lead)
         if tb < n_block:
-            east_sweep(last, tb, adj)
+            adj_copy(tb).wait()
+            east_sweep(last, tb, out)
 
     def fill_later(j, carry):
         for hour in range(last):
@@ -427,7 +458,7 @@
     def _():
         ring_copies(1).wait_recv()
 
-    for hour in range(HOURS):
+    def set_north(hour):
         here = north_sel[hour].astype(F32)
         below = ring_c[0, hour].astype(F32)
         above = ring_c[1, hour].astype(F32)
@@ -442,6 +473,7 @@
         coef_n[hour, 3] = jnp.where(even, w_p1, w_m1)
         coef_n[hour, 4] = jnp.where(even, w_m1, w_p1)
 
+    set_north(last)
     bulk = n_chunk - 2
     surface = jnp.zeros((8, width), F32)
     for hour in reversed(range(HOURS)):
@@ -455,6 +487,9 @@
         for tb in range(n_block):
             north_sweep(hour, tb)
             mix(hour, tb, 0, bulk)
+        if hour > 0:
+            set_east(hour - 1)
+            set_north(hour - 1)
         for j in range(bulk, n_chunk):
             receive(hour, j)
             widen(hour, j)
@@ -466,6 +501,8 @@
                     surface = surface + out[tb * block + i, 0:8, :]
                 if hour > 0:
                     east_sweep(hour - 1, tb, out)
+                else:
+                    out_copy(tb).start()
 
     grad_all[me] = surface
 
@@ -512,6 +549,8 @@
         return carry
 
     lax.fori_loop(0, n_chunk, drain, 0)
+    for tb in range(n_block):
+        out_copy(tb).wait()
     for k in range(1, n):
         grad_copy(k).wait_recv()
     for k in range(1, n):
@@ -546,6 +585,7 @@
     n_stage = n.bit_length() - 2
     scale = 1.0 / math.sqrt(tracers * n)
     vmem = pl.BlockSpec(memory_space=pltpu.VMEM)
+    hbm = pl.BlockSpec(memory_space=pl.ANY)
     smem = pl.BlockSpec(memory_space=pltpu.SMEM)
     dma = pltpu.SemaphoreType.DMA
     body = functools.partial(
@@ -557,9 +597,11 @@
             jax.ShapeDtypeStruct((tracers, height, width), F32),
             jax.ShapeDtypeStruct((rows, width), F32),
         ),
-        in_specs=[vmem] * 4 + [smem] * 6,
-        out_specs=(vmem, vmem),
+        in_specs=[hbm, vmem, vmem, hbm] + [smem] * 6,
+        out_specs=(hbm, vmem),
         scratch_shapes=[
+            pltpu.VMEM((tracers, height, width), F32),
+            pltpu.VMEM((half, height, width), BF16),
             pltpu.VMEM((n, 2, height, width), BF16),
             pltpu.VMEM((2, HOURS, height, width), BF16),
             pltpu.VMEM((HOURS, height, width), BF16),
@@ -591,6 +633,9 @@
             dma((HOURS, n_chunk)),
             dma((n,)),
             dma((n,)),
+            dma((n_chunk,)),
+            dma((n_block,)),
+            dma((n_block,)),
         ],
         compiler_params=pltpu.CompilerParams(
             collective_id=0, has_side_effects=True, vmem_limit_bytes=VMEM_LIMIT

time: 73.8 us -> 73.6 us (level)
  no operation moved by 1% of the time
where the time goes in v3:
time: 73.6 us; the launch traced here: 72.2 us
  Pallas kernels  67.2 us (91%)
  local copies, waits for them, and re-layouts  4.3 us (6%)
    pallas_call x1, Pallas kernels, on_device(): pl.pallas_call(body, out_shape=(jax.ShapeDtypeStruct((tracers, height, wi...  67.2 us
    unnamed x5, local copies, waits for them, and re-layouts  4.3 us

profile of v3, /device:TPU:9, one launch (start us, length us, event | category | flops | bytes accessed | tf_op | source)
XLA Modules:
  0.0 72.2 jit_solution(10340373307355747634)
XLA Ops:
  0.6 1.3 %copy.12.owner_table = s32[4,2]{1,0:T(4,128)} copy(s32[4,2]{0,1:T(2,128)} %param.14) | data formatting | bytes 64 | tf_op args[4]
  2.0 67.2 %shard_map.113 = (f32[20,120,128]{2,1,0:T(8,128)}, f32[2,128]{1,0:T(2,128)}) custom-call(f32[20,120,128]{2,1,0:T(8,128)} %bitcast.6, bf16[1,120,128]{2,1,0:T(8,128)(2,1)} %bitcast.8, bf16[1,120,128]{2,1,0:T(8,128)(2,1)} %bitcast.9, bf16[60,120,128]{2,1,0:T(8,128)(2,1)} %bitcast.5, s32[4,2]{1,0:T(4,128)} %copy.12.owner_table, s32[20]{0:T(128)} %obs_lat.1, ...), custom_call_target="tpu_custom_call" | custom-call | tf_op jit(solution)/shard_map/pallas_call | solution.py:594
  69.2 0.0 copy-start
  69.2 2.4 %copy.15 = f32[20,60,2,128]{3,2,1,0:T(2,128)} copy(f32[20,60,2,128]{3,2,1,0:T(2,128)} %bitcast.7) | data formatting | bytes 2457600
  71.6 0.0 copy-done
  71.6 0.6 copy.16
Async XLA Ops:
  69.2 2.4 %copy-start = (f32[2,128]{1,0:T(2,128)S(1)}, f32[2,128]{1,0:T(2,128)}, u32[]{:S(2)}) copy-start(f32[2,128]{1,0:T(2,128)} %get-tuple-element.9) | copy-start | bytes 3076
